TPU v7x, 32 devices: a whole 2x2x4 slice. The times are simulated.
32 devices in a mesh: dp: 8 (over z, y), ctx: 4 (over x, core).
Axes of the slice: x: 2, y: 2, z: 4, core: 2. Of those that a mesh axis runs over, the one named last changes fastest.
Arguments:
- embeds: bfloat16 [8, 512, 4096], P('dp', 'ctx'), may hold values from -6 to 6
- norm_gain: float32 [4096], replicated, may hold values from 0.1 to 1.9
- w_key: bfloat16 [4096, 512], P('dp'), may hold values from -0.09375 to 0.09375
- w_value: bfloat16 [4096, 512], P('dp'), may hold values from -0.09375 to 0.09375
- queries: bfloat16 [8, 512, 4096], P('dp', 'ctx'), may hold values from -85 to 85
- d_out: bfloat16 [8, 512, 4096], P('dp', 'ctx'), may hold values from -6 to 6
- block_doc: int32 [8, 4], P('dp'), may hold values from 0 to 2, never falling along the last dimension, each value on 1 to 2 neighbouring positions
- slot_order: int32 [8, 8], P('dp'), may hold values from 0 to 7, each once within a row
Outputs:
- grad_embed: bfloat16 [8, 512, 4096], P('dp', 'ctx')
Inputs may be any that keep to these rules, and one draw needn't show every extreme that they name: `block_doc`: along the blocks of a sequence the document number never falls; each of the 3 documents covers 1 to 2 blocks, and one covers exactly 2. `slot_order`: each row holds every number from 0 to 7 once.
All inputs are finite; a program needn't handle non-finite values.
Results may differ from a plain program's by a relative error of at most 0.035.
The roundings to bfloat16 on the way count: a program that leaves them out, or rounds other values in their place, can miss the bound.
Values may be sent and summed in bfloat16 or wider, within the bound.
A program may use at most 192 MiB of HBM per device.

v0:
```python
import jax
import jax.numpy as jnp
from jax import lax
from jax.sharding import PartitionSpec as P

HEADS = 32
KV_HEADS = 4
HEAD = 128
DOC_BLOCK = 128


def attend(query_group, dout_group, key_group, value_group, allowed, block_width, score_scale):
    tok_rows, group_size, head_size = query_group.shape
    seq_len = key_group.shape[0]
    block_count = seq_len // block_width
    mask_blocks = allowed.reshape(tok_rows, block_count, block_width)
    live_blocks = jnp.any(mask_blocks, axis=(0, 2))
    mask_blocks = mask_blocks.transpose(1, 0, 2)
    key_blocks = key_group.reshape(block_count, block_width, head_size)
    value_blocks = value_group.reshape(block_count, block_width, head_size)

    def score_block(block_item):
        is_live, key_block, mask_block = block_item
        raw_scores = jnp.einsum(
            "thd,kd->htk", query_group, key_block, preferred_element_type=jnp.float32
        )
        return jnp.where(mask_block[None], raw_scores * score_scale, -jnp.inf)

    scores = lax.map(score_block, (live_blocks, key_blocks, mask_blocks))
    row_max = jnp.max(scores, axis=(0, 3))
    raised = jnp.exp(scores - row_max[None, :, :, None])
    soft_probs = raised / jnp.sum(raised, axis=(0, 3))[None, :, :, None]
    probs_half = soft_probs.astype(jnp.bfloat16)

    def output_block(block_item):
        is_live, prob_half, value_block = block_item
        return jnp.einsum("htk,kd->htd", prob_half, value_block, preferred_element_type=jnp.float32)

    attn_out = jnp.sum(lax.map(output_block, (live_blocks, probs_half, value_blocks)), axis=0)
    row_delta = jnp.einsum("htd,thd->ht", attn_out, dout_group.astype(jnp.float32))

    def grad_block(block_item):
        is_live, prob_block, prob_half, key_block, value_block = block_item
        dprobs = jnp.einsum(
            "thd,kd->htk", dout_group, value_block, preferred_element_type=jnp.float32
        )
        score_grad = (prob_block * (dprobs - row_delta[..., None]) * score_scale).astype(
            jnp.bfloat16
        )
        key_grad = jnp.einsum(
            "htk,thd->kd", score_grad, query_group, preferred_element_type=jnp.float32
        )
        value_grad = jnp.einsum(
            "htk,thd->kd", prob_half, dout_group, preferred_element_type=jnp.float32
        )
        return (key_grad, value_grad)

    key_grad, value_grad = lax.map(
        grad_block, (live_blocks, soft_probs, probs_half, key_blocks, value_blocks)
    )
    return (key_grad.reshape(seq_len, head_size), value_grad.reshape(seq_len, head_size))


def body(embeds, norm_gain, w_key, w_value, queries, d_out, block_doc, slot_order):
    embed_rows = embeds[0]
    tok_rows = embed_rows.shape[0]
    ctx_ways = lax.axis_size("ctx")
    seq_len = tok_rows * ctx_ways
    half_len = tok_rows // 2
    kv_width = KV_HEADS * HEAD
    group_size = HEADS // KV_HEADS
    score_scale = HEAD ** (-0.5)
    as_float = embed_rows.astype(jnp.float32)
    inv_rms = lax.rsqrt(jnp.mean(as_float * as_float, axis=-1, keepdims=True) + 1e-05)
    normed = (as_float * inv_rms * norm_gain).astype(jnp.bfloat16)
    pieces = (
        lax.all_gather(w_key, "dp", axis=0, tiled=True),
        lax.all_gather(w_value, "dp", axis=0, tiled=True),
    )
    key_proj = jnp.dot(normed, pieces[0], preferred_element_type=jnp.float32)
    value_proj = jnp.dot(normed, pieces[1], preferred_element_type=jnp.float32)
    local_kv = jnp.concatenate([key_proj, value_proj], axis=1).astype(jnp.bfloat16)
    all_kv = lax.all_gather(local_kv, "ctx", axis=0, tiled=True)
    row_ids = jnp.arange(seq_len, dtype=jnp.int32)
    slot_hit = (row_ids // half_len)[:, None] == jnp.arange(2 * ctx_ways, dtype=jnp.int32)[None, :]
    key_pos = (
        jnp.sum(jnp.where(slot_hit, slot_order[0][None, :], 0), axis=1) * half_len
        + row_ids % half_len
    )
    block_hit = (key_pos // DOC_BLOCK)[:, None] == jnp.arange(block_doc.shape[1], dtype=jnp.int32)[
        None, :
    ]
    key_doc = jnp.sum(jnp.where(block_hit, block_doc[0][None, :], 0), axis=1)
    row_start = lax.axis_index("ctx") * tok_rows
    query_pos = lax.dynamic_slice_in_dim(key_pos, row_start, tok_rows)
    query_doc = lax.dynamic_slice_in_dim(key_doc, row_start, tok_rows)
    allowed = (key_pos[None, :] <= query_pos[:, None]) & (key_doc[None, :] == query_doc[:, None])
    key_grads = []
    value_grads = []
    for kv_head in range(KV_HEADS):
        first_col = kv_head * group_size * HEAD
        last_col = (kv_head + 1) * group_size * HEAD
        query_group = queries[0][:, first_col:last_col].reshape(tok_rows, group_size, HEAD)
        dout_group = d_out[0][:, first_col:last_col].reshape(tok_rows, group_size, HEAD)
        key_group = all_kv[:, kv_head * HEAD : (kv_head + 1) * HEAD]
        value_group = all_kv[:, kv_width + kv_head * HEAD : kv_width + (kv_head + 1) * HEAD]
        key_grad, value_grad = attend(
            query_group, dout_group, key_group, value_group, allowed, seq_len, score_scale
        )
        key_grads.append(key_grad)
        value_grads.append(value_grad)
    grad_terms = jnp.concatenate(key_grads + value_grads, axis=1)
    own_sum = lax.psum_scatter(
        grad_terms.astype(jnp.bfloat16), "ctx", scatter_dimension=0, tiled=True
    )
    key_half = own_sum[:, :kv_width]
    value_half = own_sum[:, kv_width:]
    contract = (((1,), (1,)), ((), ()))
    pieces = lax.all_gather((w_key, w_value), "dp", axis=0, tiled=True)
    grad_normed = lax.dot_general(
        key_half, pieces[0], contract, preferred_element_type=jnp.float32
    ) + lax.dot_general(value_half, pieces[1], contract, preferred_element_type=jnp.float32)
    mean_term = jnp.mean(as_float * norm_gain * grad_normed, axis=-1, keepdims=True)
    grad_embed = (
        inv_rms * norm_gain * grad_normed - as_float * inv_rms * inv_rms * inv_rms * mean_term
    )
    return grad_embed.astype(jnp.bfloat16)[None]


def solution(mesh):
    in_specs = (
        P("dp", "ctx", None),
        P(),
        P("dp", None),
        P("dp", None),
        P("dp", "ctx", None),
        P("dp", "ctx", None),
        P("dp", None),
        P("dp", None),
    )
    out_specs = P("dp", "ctx", None)
    return jax.shard_map(body, mesh=mesh, in_specs=in_specs, out_specs=out_specs, check_vma=False)
```

profile of v0, /device:TPU:1, one launch (start us, length us, event | category | flops | bytes accessed | tf_op | source)
XLA Modules:
  0.0 256.4 jit_solution(15721658898336120744)
XLA Ops:
  6.5 0.7 all-gather.6.cloned.1.call-update
  8.1 1.5 fusion.11
  9.6 74.2 %all-gather.6.cloned.1.call-done = bf16[4096,512]{1,0:T(8,128)(2,1)} async-done(((bf16[512,512]{1,0:T(8,128)(2,1)}), bf16[4096,512]{1,0:T(8,128)(2,1)}) %all-gather.6.cloned.1.call-update) | async-done | bytes 4194320 | tf_op jit(solution)/shard_map/all_gather | solution.py:78
  83.8 3.0 %convolution_convert_fusion = bf16[128,512]{1,0:T(8,128)(2,1)S(1)} fusion(bf16[4096,512]{1,0:T(8,128)(2,1)} %all-gather.6.cloned.1.call-done, bf16[1,128,4096]{2,1,0:T(8,128)(2,1)S(1)} %copy-done, f32[4096]{0:T(1024)S(1)} %copy-done.10, f32[128]{0:T(128)S(1)} %add_rsqrt_fusion), kind=kOutput, calls=%fused_computation.78 | convolution fusion | flops 539033600 | bytes 5390848 | tf_op jit(solution)/shard_map/dot_general | solution.py:81
  86.8 70.8 %all-gather.4.cloned.1.call-done = bf16[4096,512]{1,0:T(8,128)(2,1)} async-done(((bf16[512,512]{1,0:T(8,128)(2,1)}), bf16[4096,512]{1,0:T(8,128)(2,1)}) %all-gather.4.cloned.1.call-update) | async-done | bytes 4194320 | tf_op jit(solution)/shard_map/all_gather | solution.py:77
  157.6 2.9 %convolution_convert_fusion.1 = bf16[128,512]{1,0:T(8,128)(2,1)S(1)} fusion(bf16[4096,512]{1,0:T(8,128)(2,1)} %all-gather.4.cloned.1.call-done, bf16[1,128,4096]{2,1,0:T(8,128)(2,1)S(1)} %copy-done, f32[4096]{0:T(1024)S(1)} %copy-done.10, f32[128]{0:T(128)S(1)} %add_rsqrt_fusion), kind=kOutput, calls=%fused_computation.79 | convolution fusion | flops 539033600 | bytes 5390848 | tf_op jit(solution)/shard_map/dot_general | solution.py:80
  160.6 0.7 pad_maximum_fusion
  162.1 1.8 copy.87
  164.5 0.9 fusion.132
  165.4 0.9 fusion.131
  166.3 11.8 %all-gather.8.cloned.1.call-done = bf16[512,1024]{1,0:T(8,128)(2,1)} async-done(((bf16[128,1024]{1,0:T(8,128)(2,1)}), bf16[512,1024]{1,0:T(8,128)(2,1)}) %all-gather.8.cloned.1.call-update) | async-done | bytes 1048592 | tf_op jit(solution)/shard_map/all_gather | solution.py:83
  178.1 3.0 %fusion.133 = (f32[8,128]{1,0:T(8,128)S(1)}, f32[8,128,512]{1,2,0:T(8,128)}) fusion(pred[128,512]{0,1:T(8,128)(4,1)S(1)} %compare_and_fusion, bf16[128,8,128]{0,2,1:T(8,128)(2,1)S(1)} %bitcast.341, bf16[512,1024]{1,0:T(8,128)(2,1)} %all-gather.8.cloned.1.call-done), kind=kOutput, calls=%fused_computation.173 | convolution fusion | flops 136315392 | bytes 2560000 | tf_op jit(solution)/shard_map/sub | solution.py:31
  181.1 3.0 %fusion.134 = (f32[8,128]{1,0:T(8,128)S(1)}, f32[8,128,512]{1,2,0:T(8,128)}) fusion(pred[128,512]{0,1:T(8,128)(4,1)S(1)} %compare_and_fusion, bf16[128,8,128]{0,2,1:T(8,128)(2,1)S(1)} %bitcast.332, bf16[512,1024]{1,0:T(8,128)(2,1)} %all-gather.8.cloned.1.call-done), kind=kOutput, calls=%fused_computation.174 | convolution fusion | flops 136315392 | bytes 2560000 | tf_op jit(solution)/shard_map/sub | solution.py:31
  184.1 3.0 %fusion.135 = (f32[8,128]{1,0:T(8,128)S(1)}, f32[8,128,512]{1,2,0:T(8,128)}) fusion(pred[128,512]{0,1:T(8,128)(4,1)S(1)} %compare_and_fusion, bf16[128,8,128]{0,2,1:T(8,128)(2,1)S(1)} %bitcast.328, bf16[512,1024]{1,0:T(8,128)(2,1)} %all-gather.8.cloned.1.call-done), kind=kOutput, calls=%fused_computation.175 | convolution fusion | flops 136315392 | bytes 2560000 | tf_op jit(solution)/shard_map/sub | solution.py:31
  187.1 3.0 %fusion.136 = (f32[8,128]{1,0:T(8,128)S(1)}, f32[8,128,512]{1,2,0:T(8,128)}) fusion(pred[128,512]{0,1:T(8,128)(4,1)S(1)} %compare_and_fusion, bf16[128,8,128]{0,2,1:T(8,128)(2,1)S(1)} %bitcast.321, bf16[512,1024]{1,0:T(8,128)(2,1)} %all-gather.8.cloned.1.call-done), kind=kOutput, calls=%fused_computation.176 | convolution fusion | flops 136315392 | bytes 2560000 | tf_op jit(solution)/shard_map/sub | solution.py:31
  190.1 2.1 fusion.34
  192.2 2.0 fusion.35
  194.3 2.1 fusion.36
  196.3 2.0 fusion.37
  198.4 2.5 fusion.47
  200.9 2.5 fusion.49
  203.4 2.4 fusion.51
  205.8 2.4 fusion.53
  208.2 2.2 fusion.57
  210.4 2.1 fusion.56
  212.5 2.2 fusion.55
  214.7 2.0 fusion.54
  216.7 1.3 copy.147
  218.1 24.7 %reduce-scatter.4.cloned.1.call-done = bf16[128,1024]{1,0:T(8,128)(2,1)} async-done(((bf16[512,1024]{1,0:T(8,128)(2,1)}), bf16[128,1024]{1,0:T(8,128)(2,1)}) %reduce-scatter.4.cloned.1.call-update) | async-done | bytes 262160
  242.7 3.9 %fusion.94 = f32[128,4096]{1,0:T(8,128)S(1)} fusion(bf16[4096,512]{1,0:T(8,128)(2,1)} %all-gather.4.cloned.1.call-done, bf16[128,1024]{1,0:T(8,128)(2,1)} %reduce-scatter.4.cloned.1.call-done), kind=kOutput, calls=%fused_computation.120 | convolution fusion | flops 536870912 | bytes 6422528 | tf_op jit(solution)/shard_map/dot_general | solution.py:120
  246.6 1.6 fusion.13
  248.2 1.6 fusion.58
  (43 shorter events, 2.1 us)
Async XLA Ops:
  6.5 77.3 %copy-start = (bf16[1,128,4096]{2,1,0:T(8,128)(2,1)S(1)}, bf16[1,128,4096]{2,1,0:T(8,128)(2,1)}, u32[]{:S(2)}) copy-start(bf16[1,128,4096]{2,1,0:T(8,128)(2,1)} %param.8) | copy-start | bytes 3145732
  6.5 77.3 %copy-start.10 = (f32[4096]{0:T(1024)S(1)}, f32[4096]{0:T(1024)}, u32[]{:S(2)}) copy-start(f32[4096]{0:T(1024)} %param.9) | copy-start | bytes 49156
  6.5 77.3 %all-gather.6.cloned.1.call-start = ((), (), s32[]{:S(2)}) async-start(), calls=%async_computation.2 | async-start | bytes 4718592 | tf_op jit(solution)/shard_map/all_gather | solution.py:78
  7.3 150.4 %all-gather.4.cloned.1.call-start = ((), (), s32[]{:S(2)}) async-start(), calls=%async_computation.1 | async-start | bytes 4718592 | tf_op jit(solution)/shard_map/all_gather | solution.py:77
  8.0 170.1 %all-gather.8.cloned.1.call-start = ((), (), s32[]{:S(2)}) async-start(), calls=%async_computation.3 | async-start | bytes 1310720 | tf_op jit(solution)/shard_map/all_gather | solution.py:83
  86.8 74.6 %copy-start.2 = (bf16[1,128,4096]{2,1,0:T(8,128)(2,1)S(1)}, bf16[1,128,4096]{2,1,0:T(8,128)(2,1)}, u32[]{:S(2)}) copy-start(bf16[1,128,4096]{2,1,0:T(8,128)(2,1)} %param.12) | copy-start | bytes 3145732
  161.4 81.4 %reduce-scatter.4.cloned.1.call-start = ((), (), s32[]{:S(2)}) async-start(), calls=%async_computation.4 | async-start | bytes 1310720
  161.4 2.5 copy-start.11
  161.4 2.6 %copy-start.12 = (s32[1,4]{1,0:T(1,128)S(1)}, s32[1,4]{1,0:T(1,128)}, u32[]{:S(2)}) copy-start(s32[1,4]{1,0:T(1,128)} %param.14) | copy-start | bytes 52
  165.4 12.7 %copy-start.6 = (bf16[128,1024]{0,1:T(8,128)(2,1)S(1)}, bf16[128,1024]{0,1:T(8,128)(2,1)}, u32[]{:S(2)}) copy-start(bf16[128,1024]{0,1:T(8,128)(2,1)} %get-tuple-element.166) | copy-start | bytes 786436
  166.3 14.8 %copy-start.5 = (bf16[128,1024]{0,1:T(8,128)(2,1)S(1)}, bf16[128,1024]{0,1:T(8,128)(2,1)}, u32[]{:S(2)}) copy-start(bf16[128,1024]{0,1:T(8,128)(2,1)} %get-tuple-element.165) | copy-start | bytes 786436
  181.1 3.0 %copy-start.4 = (bf16[128,1024]{0,1:T(8,128)(2,1)S(1)}, bf16[128,1024]{0,1:T(8,128)(2,1)}, u32[]{:S(2)}) copy-start(bf16[128,1024]{0,1:T(8,128)(2,1)} %get-tuple-element.164) | copy-start | bytes 786436
  187.1 3.0 %copy-start.7 = (bf16[128,1024]{0,1:T(8,128)(2,1)S(1)}, bf16[128,1024]{0,1:T(8,128)(2,1)}, u32[]{:S(2)}) copy-start(bf16[128,1024]{0,1:T(8,128)(2,1)} %get-tuple-element.166) | copy-start | bytes 786436
  187.1 3.0 %copy-start.9 = (bf16[128,1024]{0,1:T(8,128)(2,1)S(1)}, bf16[128,1024]{0,1:T(8,128)(2,1)}, u32[]{:S(2)}) copy-start(bf16[128,1024]{0,1:T(8,128)(2,1)} %get-tuple-element.157) | copy-start | bytes 786436
  190.1 2.1 copy-start.8
  242.7 3.9 %copy-start.1 = (bf16[4096,512]{1,0:T(8,128)(2,1)S(1)}, bf16[4096,512]{1,0:T(8,128)(2,1)}, u32[]{:S(2)}) copy-start(bf16[4096,512]{1,0:T(8,128)(2,1)} %all-gather.6.cloned.1.call-done) | copy-start | bytes 12582916
  242.7 3.9 %copy-start.3 = (bf16[128,1024]{1,0:T(8,128)(2,1)S(1)}, bf16[128,1024]{1,0:T(8,128)(2,1)}, u32[]{:S(2)}) copy-start(bf16[128,1024]{1,0:T(8,128)(2,1)} %reduce-scatter.4.cloned.1.call-done) | copy-start | bytes 786436
Sparse Core Ops, SparseCore 0:
  9.5 74.2 all-gather.5
  85.9 71.6 all-gather.3
  161.5 16.5 all-gather.7
  218.2 24.4 reduce-scatter.3
where the time goes:
time: 258 us; the launch traced here: 256 us
  waiting for transfers between devices  183 us (71%)
  matrix products  49.9 us (19%)
  between operations  13.4 us (5%)
  local copies, waits for them, and re-layouts  5.79 us (2%)
  other arithmetic  4.28 us (2%)
    all_gather x1, waiting for transfers between devices, body(): lax.all_gather(w_value, 'dp', axis=0, tiled=True)  74.2 us
    all_gather x1, waiting for transfers between devices, body(): lax.all_gather(w_key, 'dp', axis=0, tiled=True)  70.8 us
    unnamed x5, waiting for transfers between devices  26.1 us
    sub x4, matrix products, attend(): raised = jnp.exp(scores - row_max[None, :, :, None])  12 us
    all_gather x1, waiting for transfers between devices, body(): all_kv = lax.all_gather(local_kv, 'ctx', axis=0, tiled=True)  11.8 us
    dot_general x4, matrix products, grad_block(): jnp.einsum('htk,thd->kd', score_grad, query_group, preferred_element_type...  9.73 us
    dot_general x4, matrix products, grad_block(): jnp.einsum('htk,thd->kd', prob_half, dout_group, preferred_element_type=j...  8.55 us
    unnamed x4, matrix products  8.24 us
  transfers between devices with their start and end apart: 4, of which 4 were waited for; matrix products, arithmetic and copies ran while one was open for 4% of the time, Pallas kernels for 0%

commit v1 on v0

v1 whole, which is shorter than its diff:
```python
import functools
import math

import jax
import jax.numpy as jnp
from jax import lax
from jax.experimental import pallas as pl
from jax.experimental.pallas import tpu as pltpu
from jax.sharding import PartitionSpec as P

HEADS = 32
KV_HEADS = 4
HEAD = 128
GROUP = HEADS // KV_HEADS
DOC_BLOCK = 128
MESH = pl.DeviceIdType.MESH
F32 = jnp.float32
BF16 = jnp.bfloat16
NT = (((1,), (1,)), ((), ()))


def kernel(
    dp_ways,
    ctx_ways,
    wk_ref,
    wv_ref,
    emb_ref,
    gain_ref,
    q_ref,
    do_ref,
    bias_ref,
    out_ref,
    wg,
    wo,
    n2,
    kv,
    gs,
    rs,
    gn,
    dk_acc,
    dv_acc,
    w_send,
    w_recv,
    n_send,
    n_recv,
    wo_send,
    wo_recv,
    kv_send,
    kv_recv,
    g_send,
    g_recv,
):
    toks, dim = emb_ref.shape
    rows = dim // dp_ways
    line = dp_ways // 2
    chips = ctx_ways // 2
    splits = 2 if chips == 2 else 1
    part = rows // splits
    seq = toks * ctx_ways

    dp = lax.axis_index("dp")
    ctx = lax.axis_index("ctx")
    za, yb = dp // 2, dp % 2
    chip, core = ctx // 2, ctx % 2
    mine = chip % splits
    other = splits - 1 - mine
    partner = chip * 2 + 1 - core
    y_dp = za * 2 + 1 - yb
    x_ctx = (chips - 1 - chip) * 2 + core
    has_up, has_down = za + 1 < line, za >= 1
    sends = []

    def send(copy, cond=None):
        if cond is None:
            copy.start()
        else:
            pl.when(cond)(copy.start)
        sends.append((copy, cond))

    barrier = pltpu.get_barrier_semaphore()

    def greet(where):
        pl.semaphore_signal(barrier, inc=1, device_id=where, device_id_type=MESH)

    for step in range(1, ctx_ways):
        greet((dp, lax.rem(ctx + step, ctx_ways)))
    greet((y_dp, ctx))
    pl.when(has_up)(lambda: greet((dp + 2, ctx)))
    pl.when(has_down)(lambda: greet((dp - 2, ctx)))

    @pl.when(core == 0)
    def _():
        for h in range(KV_HEADS):
            wg[h, dp] = wk_ref[:, h * HEAD : (h + 1) * HEAD]

    @pl.when(core == 1)
    def _():
        for h in range(KV_HEADS):
            wg[h, dp] = wv_ref[:, h * HEAD : (h + 1) * HEAD]

    pl.semaphore_wait(
        barrier, ctx_ways + jnp.where(has_up, 1, 0) + jnp.where(has_down, 1, 0)
    )

    def piece(h, p, s):
        return wg.at[h, p, pl.ds(pl.multiple_of(s * part, part), part)]

    def w_copy(h, p, s, slot, where):
        return pltpu.make_async_remote_copy(
            src_ref=piece(h, p, s),
            dst_ref=piece(h, p, s),
            send_sem=w_send.at[h, p, slot],
            recv_sem=w_recv.at[h, p, s],
            device_id=where,
            device_id_type=MESH,
        )

    up, down, ybor, xbor = (dp + 2, ctx), (dp - 2, ctx), (y_dp, ctx), (dp, x_ctx)

    for h in range(KV_HEADS):
        send(w_copy(h, dp, mine, 0, up), has_up)
        send(w_copy(h, dp, mine, 1, down), has_down)
        send(w_copy(h, dp, mine, 2, ybor))
        if splits == 2:
            send(w_copy(h, dp, other, 3, ybor))

    step_cols = 512
    col_steps = dim // step_cols
    total = jnp.zeros((toks, 1), F32)
    for k in range(col_steps):
        e = emb_ref[:, k * step_cols : (k + 1) * step_cols].astype(F32)
        total += jnp.sum(e * e, axis=1, keepdims=True)
    inv_rms = lax.rsqrt(total * (1.0 / dim) + 1e-05)
    for k in range(col_steps):
        cols = slice(k * step_cols, (k + 1) * step_cols)
        e = emb_ref[:, cols].astype(F32)
        n2[core, :, cols] = (e * inv_rms * gain_ref[:, cols]).astype(BF16)
    n_copy = pltpu.make_async_remote_copy(
        src_ref=n2.at[core],
        dst_ref=n2.at[core],
        send_sem=n_send,
        recv_sem=n_recv,
        device_id=(dp, partner),
        device_id_type=MESH,
    )
    send(n_copy)

    def gather(h):
        for d in range(1, line):
            lo, hi = dp - 2 * d, dp + 2 * d
            lo_in, hi_in = za >= d, za + d < line

            @pl.when(lo_in)
            def _():
                w_copy(h, lo, mine, 0, up).wait_recv()

            send(w_copy(h, lo, mine, 0, up), lo_in & has_up)
            send(w_copy(h, lo, mine, 2, ybor), lo_in)
            if splits == 2:
                send(w_copy(h, lo, mine, 3, xbor), lo_in)

            @pl.when(hi_in)
            def _():
                w_copy(h, hi, mine, 0, up).wait_recv()

            send(w_copy(h, hi, mine, 1, down), hi_in & has_down)
            send(w_copy(h, hi, mine, 2, ybor), hi_in)
            if splits == 2:
                send(w_copy(h, hi, mine, 3, xbor), hi_in)
        w_copy(h, y_dp, mine, 0, up).wait_recv()
        if splits == 2:
            w_copy(h, y_dp, other, 0, up).wait_recv()
        for d in range(1, line):
            for far, inside in ((y_dp - 2 * d, za >= d), (y_dp + 2 * d, za + d < line)):

                @pl.when(inside)
                def _(far=far):
                    w_copy(h, far, mine, 0, up).wait_recv()

                if splits == 2:
                    send(w_copy(h, far, mine, 3, xbor), inside)
        if splits == 2:
            for d in range(1, line):
                for base in (dp, y_dp):
                    for far, inside in ((base - 2 * d, za >= d), (base + 2 * d, za + d < line)):

                        @pl.when(inside)
                        def _(far=far):
                            w_copy(h, far, other, 0, up).wait_recv()

    def project(h):
        acc = jnp.zeros((2 * toks, HEAD), F32)
        for p in range(dp_ways):
            x = n2[:, :, p * rows : (p + 1) * rows].reshape(2 * toks, rows)
            acc += jnp.dot(x, wg[h, p], preferred_element_type=F32)
        kv[core, h, pl.ds(chip * 2, 2)] = acc.astype(BF16).reshape(2, toks, HEAD)
        for step in range(1, ctx_ways):
            send(
                pltpu.make_async_remote_copy(
                    src_ref=kv.at[core, h, pl.ds(chip * 2, 2)],
                    dst_ref=kv.at[core, h, pl.ds(chip * 2, 2)],
                    send_sem=kv_send.at[h, step],
                    recv_sem=kv_recv.at[h, ctx],
                    device_id=(dp, lax.rem(ctx + step, ctx_ways)),
                    device_id_type=MESH,
                )
            )
        send(
            pltpu.make_async_remote_copy(
                src_ref=wg.at[h],
                dst_ref=wo.at[h],
                send_sem=wo_send.at[h],
                recv_sem=wo_recv.at[h],
                device_id=(dp, partner),
                device_id_type=MESH,
            )
        )

    wide = 2 if seq <= 512 else 1
    scale = HEAD ** (-0.5)

    def attend(h):
        for step in range(1, ctx_ways):
            src = lax.rem(ctx + step, ctx_ways)
            at = (src // 2) * 2
            blk = kv.at[src % 2, h, pl.ds(at, 2)]
            pltpu.make_async_remote_copy(
                src_ref=blk,
                dst_ref=blk,
                send_sem=kv_send.at[h, step],
                recv_sem=kv_recv.at[h, src],
                device_id=(dp, src),
                device_id_type=MESH,
            ).wait_recv()
        dk_acc[...] = jnp.zeros_like(dk_acc)
        dv_acc[...] = jnp.zeros_like(dv_acc)

        def chunk(i, carry):
            first = (h * GROUP + i * wide) * HEAD

            def take(ref):
                cuts = [
                    ref[:, pl.ds(pl.multiple_of(first + w * HEAD, HEAD), HEAD)]
                    for w in range(wide)
                ]
                return jnp.concatenate(cuts, axis=0) if wide > 1 else cuts[0]

            q, do = take(q_ref), take(do_ref)
            keys = kv[0, h].reshape(seq, HEAD)
            vals = kv[1, h].reshape(seq, HEAD)
            bias = bias_ref[...]
            if wide > 1:
                bias = jnp.concatenate([bias] * wide, axis=1)
            s = lax.dot_general(keys, q, NT, preferred_element_type=F32) + bias
            top = jnp.max(s, axis=0, keepdims=True)
            raised = jnp.exp2((s - top) * (scale * math.log2(math.e)))
            probs = raised * (1.0 / jnp.sum(raised, axis=0, keepdims=True))
            half = probs.astype(BF16)
            dpr = lax.dot_general(vals, do, NT, preferred_element_type=F32)
            delta = jnp.sum(half.astype(F32) * dpr, axis=0, keepdims=True)
            sg = (probs * (dpr - delta) * scale).astype(BF16)
            dk_acc[...] += jnp.dot(sg, q, preferred_element_type=F32)
            dv_acc[...] += jnp.dot(half, do, preferred_element_type=F32)
            return carry

        lax.fori_loop(0, GROUP // wide, chunk, 0)
        gs[h, :, 0] = dk_acc[...].astype(BF16).reshape(ctx_ways, toks, HEAD)
        gs[h, :, 1] = dv_acc[...].astype(BF16).reshape(ctx_ways, toks, HEAD)
        for step in range(1, ctx_ways):
            dst = lax.rem(ctx + step, ctx_ways)
            send(
                pltpu.make_async_remote_copy(
                    src_ref=gs.at[h, dst],
                    dst_ref=rs.at[h, ctx],
                    send_sem=g_send.at[h, step],
                    recv_sem=g_recv.at[h, ctx],
                    device_id=(dp, dst),
                    device_id_type=MESH,
                )
            )

    def backward(h):
        for step in range(1, ctx_ways):
            src = lax.rem(ctx + step, ctx_ways)
            pltpu.make_async_remote_copy(
                src_ref=gs.at[h, src],
                dst_ref=rs.at[h, src],
                send_sem=g_send.at[h, step],
                recv_sem=g_recv.at[h, src],
                device_id=(dp, src),
                device_id_type=MESH,
            ).wait_recv()
        pltpu.make_async_remote_copy(
            src_ref=wg.at[h],
            dst_ref=wo.at[h],
            send_sem=wo_send.at[h],
            recv_sem=wo_recv.at[h],
            device_id=(dp, partner),
            device_id_type=MESH,
        ).wait_recv()
        own = gs[h, ctx, core].astype(F32)
        cross = gs[h, ctx, 1 - core].astype(F32)
        for step in range(1, ctx_ways):
            src = lax.rem(ctx + step, ctx_ways)
            own += rs[h, src, core].astype(F32)
            cross += rs[h, src, 1 - core].astype(F32)
        own, cross = own.astype(BF16), cross.astype(BF16)
        for p in range(dp_ways):
            cols = slice(p * rows, (p + 1) * rows)
            term = lax.dot_general(own, wg[h, p], NT, preferred_element_type=F32)
            term += lax.dot_general(cross, wo[h, p], NT, preferred_element_type=F32)
            if h == 0:
                gn[:, cols] = term
            else:
                gn[:, cols] += term

    for h in range(KV_HEADS):
        gather(h)
        if h == 0:
            pltpu.make_async_remote_copy(
                src_ref=n2.at[1 - core],
                dst_ref=n2.at[1 - core],
                send_sem=n_send,
                recv_sem=n_recv,
                device_id=(dp, partner),
                device_id_type=MESH,
            ).wait_recv()
        project(h)
        if h >= 1:
            attend(h - 1)
        if h >= 2:
            backward(h - 2)
    attend(KV_HEADS - 1)
    if KV_HEADS >= 2:
        backward(KV_HEADS - 2)
    backward(KV_HEADS - 1)

    total = jnp.zeros((toks, 1), F32)
    for k in range(col_steps):
        cols = slice(k * step_cols, (k + 1) * step_cols)
        total += jnp.sum(
            emb_ref[:, cols].astype(F32) * gain_ref[:, cols] * gn[:, cols], axis=1, keepdims=True
        )
    shift = inv_rms * inv_rms * inv_rms * (total * (1.0 / dim))
    for k in range(col_steps):
        cols = slice(k * step_cols, (k + 1) * step_cols)
        e = emb_ref[:, cols].astype(F32)
        out_ref[:, cols] = (inv_rms * gain_ref[:, cols] * gn[:, cols] - e * shift).astype(BF16)

    for copy, cond in sends:
        if cond is None:
            copy.wait_send()
        else:
            pl.when(cond)(copy.wait_send)


def body(embeds, norm_gain, w_key, w_value, queries, d_out, block_doc, slot_order):
    embed_rows = embeds[0]
    toks, dim = embed_rows.shape
    dp_ways = lax.axis_size("dp")
    ctx_ways = lax.axis_size("ctx")
    seq = toks * ctx_ways
    half_len = seq // slot_order.shape[1]
    rows = dim // dp_ways
    row_ids = jnp.arange(seq, dtype=jnp.int32)
    slot_hit = (row_ids // half_len)[:, None] == jnp.arange(slot_order.shape[1], dtype=jnp.int32)
    pos = jnp.sum(jnp.where(slot_hit, slot_order[0][None, :], 0), axis=1) * half_len
    pos = pos + row_ids % half_len
    block_hit = (pos // DOC_BLOCK)[:, None] == jnp.arange(block_doc.shape[1], dtype=jnp.int32)
    doc = jnp.sum(jnp.where(block_hit, block_doc[0][None, :], 0), axis=1)
    start = lax.axis_index("ctx") * toks
    q_pos = lax.dynamic_slice_in_dim(pos, start, toks)
    q_doc = lax.dynamic_slice_in_dim(doc, start, toks)
    allowed = (pos[:, None] <= q_pos[None, :]) & (doc[:, None] == q_doc[None, :])
    bias = jnp.where(allowed, 0.0, -jnp.inf).astype(F32)

    vmem = pl.BlockSpec(memory_space=pltpu.VMEM)
    dma = pltpu.SemaphoreType.DMA
    splits = 2
    out = pl.pallas_call(
        functools.partial(kernel, dp_ways, ctx_ways),
        out_shape=jax.ShapeDtypeStruct((toks, dim), BF16),
        in_specs=[vmem] * 7,
        out_specs=vmem,
        scratch_shapes=[
            pltpu.VMEM((KV_HEADS, dp_ways, rows, HEAD), BF16),
            pltpu.VMEM((KV_HEADS, dp_ways, rows, HEAD), BF16),
            pltpu.VMEM((2, toks, dim), BF16),
            pltpu.VMEM((2, KV_HEADS, ctx_ways, toks, HEAD), BF16),
            pltpu.VMEM((KV_HEADS, ctx_ways, 2, toks, HEAD), BF16),
            pltpu.VMEM((KV_HEADS, ctx_ways, 2, toks, HEAD), BF16),
            pltpu.VMEM((toks, dim), F32),
            pltpu.VMEM((seq, HEAD), F32),
            pltpu.VMEM((seq, HEAD), F32),
            dma((KV_HEADS, dp_ways, 4)),
            dma((KV_HEADS, dp_ways, splits)),
            dma,
            dma,
            dma((KV_HEADS,)),
            dma((KV_HEADS,)),
            dma((KV_HEADS, ctx_ways)),
            dma((KV_HEADS, ctx_ways)),
            dma((KV_HEADS, ctx_ways)),
            dma((KV_HEADS, ctx_ways)),
        ],
        compiler_params=pltpu.CompilerParams(
            collective_id=0, has_side_effects=True, vmem_limit_bytes=56 * 1024 * 1024
        ),
    )(w_key, w_value, embed_rows, norm_gain[None], queries[0], d_out[0], bias)
    return out[None]


def solution(mesh):
    in_specs = (
        P("dp", "ctx", None),
        P(),
        P("dp", None),
        P("dp", None),
        P("dp", "ctx", None),
        P("dp", "ctx", None),
        P("dp", None),
        P("dp", None),
    )
    out_specs = P("dp", "ctx", None)
    return jax.shard_map(body, mesh=mesh, in_specs=in_specs, out_specs=out_specs, check_vma=False)
```

time: 258 us -> 96 us (0.37)
  waiting for transfers between devices: 183 us -> 0 us
  Pallas kernels: 0 us -> 91 us
  matrix products: 49.9 us -> 0 us
  between operations: 13.4 us -> 0.02 us
  other arithmetic: 4.28 us -> 1.09 us
    all_gather x3 -> x0, waiting for transfers between devices: 157 us -> none  [the longest x1 74.2 us: body(): lax.all_gather(w_value, 'dp', axis=0, tiled=True)]
    pallas_call x0 -> x1, Pallas kernels: none -> 91 us  [body(): pl.pallas_call(functools.partial(kernel, dp_ways, ctx_ways), out_shape=ja...]
    dot_general x12 -> x0, matrix products: 29.6 us -> none  [the longest x4 9.73 us: grad_block(): jnp.einsum('htk,thd->kd', score_grad, query_group, preferred_element_type...]
    unnamed x5 -> x0, waiting for transfers between devices: 26.1 us -> none
    sub x4 -> x0, matrix products: 12 us -> none  [attend(): raised = jnp.exp(scores - row_max[None, :, :, None])]
    unnamed x4 -> x0, matrix products: 8.24 us -> none
  transfers between devices with their start and end apart: 4 -> 0, of which waited for: 4 -> 0; matrix products, arithmetic and copies ran while one was open for 4% -> 0% of each run, Pallas kernels for 0% -> 0%
where the time goes in v1:
time: 96 us; the launch traced here: 95.8 us
  Pallas kernels  91 us (95%)
  local copies, waits for them, and re-layouts  3.74 us (4%)
  other arithmetic  1.09 us (1%)
    pallas_call x1, Pallas kernels, body(): pl.pallas_call(functools.partial(kernel, dp_ways, ctx_ways), out_shape=ja...  91 us
    unnamed x5, local copies, waits for them, and re-layouts  3.59 us

profile of v1, /device:TPU:1, one launch (start us, length us, event | category | flops | bytes accessed | tf_op | source)
XLA Modules:
  0.0 95.8 jit_solution(3461862616753187302)
XLA Ops:
  0.0 0.0 copy-start
  0.0 0.6 copy-done
  0.7 0.1 select_reduce_fusion
  0.8 0.0 copy-start.1
  0.8 0.6 copy-done.1
  1.4 0.1 select_reduce_fusion.1
  1.5 0.1 dynamic_slice.7
  1.6 0.1 dynamic_slice.6
  1.6 0.9 and_select_fusion.bias_ref
  2.6 91.0 %shard_map.82 = bf16[128,4096]{1,0:T(8,128)(2,1)} custom-call(bf16[512,512]{1,0:T(8,128)(2,1)} %wk_ref.1, bf16[512,512]{1,0:T(8,128)(2,1)} %wv_ref.1, bf16[128,4096]{1,0:T(8,128)(2,1)} %bitcast.8, f32[1,4096]{1,0:T(1,128)} %bitcast.11, bf16[128,4096]{1,0:T(8,128)(2,1)} %bitcast.9, bf16[128,4096]{1,0:T(8,128)(2,1)} %bitcast.10, ...), custom_call_target="tpu_custom_call" | custom-call | tf_op jit(solution)/shard_map/pallas_call | solution.py:380
  93.5 2.3 %copy.10 = bf16[1,128,4096]{2,1,0:T(8,128)(2,1)} copy(bf16[1,128,4096]{2,1,0:T(8,128)(2,1)} %bitcast.7) | data formatting | bytes 2097152
  (2 shorter events, 0.0 us)
Async XLA Ops:
  0.0 0.7 copy-start
  0.8 0.7 copy-start.1

commit v2 on v1

--- a/solution.py
+++ b/solution.py
@@ -22,14 +22,21 @@
 def kernel(
     dp_ways,
     ctx_ways,
-    wk_ref,
-    wv_ref,
+    doc_ref,
+    slot_ref,
+    wk_hbm,
+    wv_hbm,
+    emb_hbm,
+    gain_ref,
+    q_hbm,
+    do_hbm,
+    out_ref,
     emb_ref,
-    gain_ref,
     q_ref,
     do_ref,
     bias_ref,
-    out_ref,
+    load_sem,
+    own_sem,
     wg,
     wo,
     n2,
@@ -50,7 +57,7 @@
     g_send,
     g_recv,
 ):
-    toks, dim = emb_ref.shape
+    toks, dim = emb_hbm.shape
     rows = dim // dp_ways
     line = dp_ways // 2
     chips = ctx_ways // 2
@@ -88,41 +95,107 @@
     pl.when(has_up)(lambda: greet((dp + 2, ctx)))
     pl.when(has_down)(lambda: greet((dp - 2, ctx)))
 
-    @pl.when(core == 0)
-    def _():
-        for h in range(KV_HEADS):
-            wg[h, dp] = wk_ref[:, h * HEAD : (h + 1) * HEAD]
-
-    @pl.when(core == 1)
-    def _():
-        for h in range(KV_HEADS):
-            wg[h, dp] = wv_ref[:, h * HEAD : (h + 1) * HEAD]
+    def own_load(src, h):
+        return pltpu.make_async_copy(
+            src.at[:, pl.ds(h * HEAD, HEAD)], wg.at[h, dp], own_sem.at[h]
+        )
+
+    for h in range(KV_HEADS):
+        pl.when(core == 0)(own_load(wk_hbm, h).start)
+        pl.when(core == 1)(own_load(wv_hbm, h).start)
+    loads = [
+        pltpu.make_async_copy(src, dst, load_sem.at[i])
+        for i, (src, dst) in enumerate(((emb_hbm, emb_ref), (q_hbm, q_ref), (do_hbm, do_ref)))
+    ]
+    for load in loads:
+        load.start()
 
     pl.semaphore_wait(
         barrier, ctx_ways + jnp.where(has_up, 1, 0) + jnp.where(has_down, 1, 0)
     )
 
-    def piece(h, p, s):
-        return wg.at[h, p, pl.ds(pl.multiple_of(s * part, part), part)]
+    up, down, ybor, xbor = (dp + 2, ctx), (dp - 2, ctx), (y_dp, ctx), (dp, x_ctx)
 
     def w_copy(h, p, s, slot, where):
+        if s is None:
+            ref, sem = wg.at[h, p], 0
+        else:
+            ref, sem = wg.at[h, p, pl.ds(pl.multiple_of(s * part, part), part)], s
         return pltpu.make_async_remote_copy(
-            src_ref=piece(h, p, s),
-            dst_ref=piece(h, p, s),
+            src_ref=ref,
+            dst_ref=ref,
             send_sem=w_send.at[h, p, slot],
-            recv_sem=w_recv.at[h, p, s],
+            recv_sem=w_recv.at[h, p, sem],
             device_id=where,
             device_id_type=MESH,
         )
 
-    up, down, ybor, xbor = (dp + 2, ctx), (dp - 2, ctx), (y_dp, ctx), (dp, x_ctx)
-
-    for h in range(KV_HEADS):
-        send(w_copy(h, dp, mine, 0, up), has_up)
-        send(w_copy(h, dp, mine, 1, down), has_down)
-        send(w_copy(h, dp, mine, 2, ybor))
-        if splits == 2:
-            send(w_copy(h, dp, other, 3, ybor))
+    def arrive(h, p, s, cond):
+        @pl.when(cond)
+        def _():
+            w_copy(h, p, s, 0, up).wait_recv()
+
+    def start_own(h):
+        own_load(wk_hbm, h).wait()
+        send(w_copy(h, dp, None, 0, up), has_up)
+        send(w_copy(h, dp, None, 1, down), has_down)
+        send(w_copy(h, dp, None, 2, ybor))
+
+    def sides(d):
+        odd = za % 2 == 1
+        never = za < 0
+        return (
+            (-2 * d, za >= d, odd if d == 1 else never, 1),
+            (2 * d, za + d < line, jnp.logical_not(odd) if d == 1 else never, 0),
+        )
+
+    def relay(h, k):
+        if k < line:
+            for off, inside, whole, away in sides(k):
+                p = dp + off
+                arrive(h, p, None, inside)
+                if away == 1:
+                    send(w_copy(h, p, None, 0, up), inside & has_up)
+                else:
+                    send(w_copy(h, p, None, 1, down), inside & has_down)
+                if splits == 1:
+                    send(w_copy(h, p, None, 2, ybor), inside)
+                else:
+                    if k == 1:
+                        send(w_copy(h, p, None, 2, ybor), inside & whole)
+                    send(
+                        w_copy(h, p, mine, 2, ybor),
+                        inside & jnp.logical_not(whole) if k == 1 else inside,
+                    )
+        if k > 1 and splits == 2:
+            for off, inside, whole, _away in sides(k - 1):
+                p = y_dp + off
+                half = inside & jnp.logical_not(whole) if k == 2 else inside
+                arrive(h, p, mine, half)
+                send(w_copy(h, p, mine, 3, xbor), half)
+
+    def complete(h):
+        w_copy(h, y_dp, None, 0, up).wait_recv()
+        for d in range(1, line):
+            for off, inside, whole, _away in sides(d):
+                p = y_dp + off
+                if splits == 1:
+                    arrive(h, p, None, inside)
+                elif d == 1:
+                    arrive(h, p, None, inside & whole)
+                    arrive(h, p, other, inside & jnp.logical_not(whole))
+                else:
+                    arrive(h, p, other, inside)
+
+    def wave(w):
+        if w + 1 < KV_HEADS:
+            start_own(w + 1)
+        for h in range(KV_HEADS):
+            if 1 <= w - h + 1 <= line:
+                relay(h, w - h + 1)
+
+    start_own(0)
+    loads[0].wait()
 
     step_cols = 512
     col_steps = dim // step_cols
@@ -131,6 +204,7 @@
         e = emb_ref[:, k * step_cols : (k + 1) * step_cols].astype(F32)
         total += jnp.sum(e * e, axis=1, keepdims=True)
     inv_rms = lax.rsqrt(total * (1.0 / dim) + 1e-05)
+    wave(0)
     for k in range(col_steps):
         cols = slice(k * step_cols, (k + 1) * step_cols)
         e = emb_ref[:, cols].astype(F32)
@@ -145,48 +219,29 @@
     )
     send(n_copy)
 
-    def gather(h):
-        for d in range(1, line):
-            lo, hi = dp - 2 * d, dp + 2 * d
-            lo_in, hi_in = za >= d, za + d < line
-
-            @pl.when(lo_in)
-            def _():
-                w_copy(h, lo, mine, 0, up).wait_recv()
-
-            send(w_copy(h, lo, mine, 0, up), lo_in & has_up)
-            send(w_copy(h, lo, mine, 2, ybor), lo_in)
-            if splits == 2:
-                send(w_copy(h, lo, mine, 3, xbor), lo_in)
-
-            @pl.when(hi_in)
-            def _():
-                w_copy(h, hi, mine, 0, up).wait_recv()
-
-            send(w_copy(h, hi, mine, 1, down), hi_in & has_down)
-            send(w_copy(h, hi, mine, 2, ybor), hi_in)
-            if splits == 2:
-                send(w_copy(h, hi, mine, 3, xbor), hi_in)
-        w_copy(h, y_dp, mine, 0, up).wait_recv()
-        if splits == 2:
-            w_copy(h, y_dp, other, 0, up).wait_recv()
-        for d in range(1, line):
-            for far, inside in ((y_dp - 2 * d, za >= d), (y_dp + 2 * d, za + d < line)):
-
-                @pl.when(inside)
-                def _(far=far):
-                    w_copy(h, far, mine, 0, up).wait_recv()
-
-                if splits == 2:
-                    send(w_copy(h, far, mine, 3, xbor), inside)
-        if splits == 2:
-            for d in range(1, line):
-                for base in (dp, y_dp):
-                    for far, inside in ((base - 2 * d, za >= d), (base + 2 * d, za + d < line)):
-
-                        @pl.when(inside)
-                        def _(far=far):
-                            w_copy(h, far, other, 0, up).wait_recv()
+    slots = slot_ref.shape[1]
+    half_len = seq // slots
+    lane = lax.broadcasted_iota(jnp.int32, (1, toks), 1)
+    down_rows = lax.broadcasted_iota(jnp.int32, (half_len, 1), 0)
+    per_dev = toks // half_len
+
+    def slot_doc(start):
+        block, found = start // DOC_BLOCK, jnp.int32(0)
+        for i in range(doc_ref.shape[1]):
+            found = jnp.where(block == i, doc_ref[0, i], found)
+        return found
+
+    q_pos = jnp.zeros((1, toks), jnp.int32)
+    q_doc = jnp.zeros((1, toks), jnp.int32)
+    for i in range(per_dev):
+        start = slot_ref[0, ctx * per_dev + i] * half_len
+        here = (lane >= i * half_len) & (lane < (i + 1) * half_len)
+        q_pos = jnp.where(here, start + lane - i * half_len, q_pos)
+        q_doc = jnp.where(here, slot_doc(start), q_doc)
+    for j in range(slots):
+        start = slot_ref[0, j] * half_len
+        allowed = ((start + down_rows) <= q_pos) & (q_doc == slot_doc(start))
+        bias_ref[j * half_len : (j + 1) * half_len, :] = jnp.where(allowed, 0.0, -jnp.inf)
 
     def project(h):
         acc = jnp.zeros((2 * toks, HEAD), F32)
@@ -219,7 +274,7 @@
     wide = 2 if seq <= 512 else 1
     scale = HEAD ** (-0.5)
 
-    def attend(h):
+    def attend(h, between=None):
         for step in range(1, ctx_ways):
             src = lax.rem(ctx + step, ctx_ways)
             at = (src // 2) * 2
@@ -234,6 +289,9 @@
             ).wait_recv()
         dk_acc[...] = jnp.zeros_like(dk_acc)
         dv_acc[...] = jnp.zeros_like(dv_acc)
+        if h == 0:
+            loads[1].wait()
+            loads[2].wait()
 
         def chunk(i, carry):
             first = (h * GROUP + i * wide) * HEAD
@@ -263,7 +321,11 @@
             dv_acc[...] += jnp.dot(half, do, preferred_element_type=F32)
             return carry
 
-        lax.fori_loop(0, GROUP // wide, chunk, 0)
+        cut = GROUP // wide // 2
+        lax.fori_loop(0, cut, chunk, 0)
+        if between is not None:
+            between()
+        lax.fori_loop(cut, GROUP // wide, chunk, 0)
         gs[h, :, 0] = dk_acc[...].astype(BF16).reshape(ctx_ways, toks, HEAD)
         gs[h, :, 1] = dv_acc[...].astype(BF16).reshape(ctx_ways, toks, HEAD)
         for step in range(1, ctx_ways):
@@ -314,25 +376,25 @@
             else:
                 gn[:, cols] += term
 
+    for w in range(1, line + 1):
+        wave(w)
+    complete(0)
+    pltpu.make_async_remote_copy(
+        src_ref=n2.at[1 - core],
+        dst_ref=n2.at[1 - core],
+        send_sem=n_send,
+        recv_sem=n_recv,
+        device_id=(dp, partner),
+        device_id_type=MESH,
+    ).wait_recv()
     for h in range(KV_HEADS):
-        gather(h)
-        if h == 0:
-            pltpu.make_async_remote_copy(
-                src_ref=n2.at[1 - core],
-                dst_ref=n2.at[1 - core],
-                send_sem=n_send,
-                recv_sem=n_recv,
-                device_id=(dp, partner),
-                device_id_type=MESH,
-            ).wait_recv()
+        if h > 0:
+            complete(h)
         project(h)
-        if h >= 1:
-            attend(h - 1)
         if h >= 2:
             backward(h - 2)
-    attend(KV_HEADS - 1)
-    if KV_HEADS >= 2:
-        backward(KV_HEADS - 2)
+        attend(h, functools.partial(wave, line + 1 + h))
+    backward(KV_HEADS - 2)
     backward(KV_HEADS - 1)
 
     total = jnp.zeros((toks, 1), F32)
@@ -360,29 +422,24 @@
     dp_ways = lax.axis_size("dp")
     ctx_ways = lax.axis_size("ctx")
     seq = toks * ctx_ways
-    half_len = seq // slot_order.shape[1]
     rows = dim // dp_ways
-    row_ids = jnp.arange(seq, dtype=jnp.int32)
-    slot_hit = (row_ids // half_len)[:, None] == jnp.arange(slot_order.shape[1], dtype=jnp.int32)
-    pos = jnp.sum(jnp.where(slot_hit, slot_order[0][None, :], 0), axis=1) * half_len
-    pos = pos + row_ids % half_len
-    block_hit = (pos // DOC_BLOCK)[:, None] == jnp.arange(block_doc.shape[1], dtype=jnp.int32)
-    doc = jnp.sum(jnp.where(block_hit, block_doc[0][None, :], 0), axis=1)
-    start = lax.axis_index("ctx") * toks
-    q_pos = lax.dynamic_slice_in_dim(pos, start, toks)
-    q_doc = lax.dynamic_slice_in_dim(doc, start, toks)
-    allowed = (pos[:, None] <= q_pos[None, :]) & (doc[:, None] == q_doc[None, :])
-    bias = jnp.where(allowed, 0.0, -jnp.inf).astype(F32)
-
     vmem = pl.BlockSpec(memory_space=pltpu.VMEM)
+    smem = pl.BlockSpec(memory_space=pltpu.SMEM)
+    hbm = pl.BlockSpec(memory_space=pl.ANY)
     dma = pltpu.SemaphoreType.DMA
     splits = 2
     out = pl.pallas_call(
         functools.partial(kernel, dp_ways, ctx_ways),
         out_shape=jax.ShapeDtypeStruct((toks, dim), BF16),
-        in_specs=[vmem] * 7,
+        in_specs=[smem, smem, hbm, hbm, hbm, vmem, hbm, hbm],
         out_specs=vmem,
         scratch_shapes=[
+            pltpu.VMEM((toks, dim), BF16),
+            pltpu.VMEM((toks, dim), BF16),
+            pltpu.VMEM((toks, dim), BF16),
+            pltpu.VMEM((seq, toks), F32),
+            dma((3,)),
+            dma((KV_HEADS,)),
             pltpu.VMEM((KV_HEADS, dp_ways, rows, HEAD), BF16),
             pltpu.VMEM((KV_HEADS, dp_ways, rows, HEAD), BF16),
             pltpu.VMEM((2, toks, dim), BF16),
@@ -406,7 +463,9 @@
         compiler_params=pltpu.CompilerParams(
             collective_id=0, has_side_effects=True, vmem_limit_bytes=56 * 1024 * 1024
         ),
-    )(w_key, w_value, embed_rows, norm_gain[None], queries[0], d_out[0], bias)
+    )(
+        block_doc, slot_order, w_key, w_value, embed_rows, norm_gain[None], queries[0], d_out[0]
+    )
     return out[None]
 
 

time: 96 us -> 89.7 us (0.934)
  Pallas kernels: 91 us -> 87.2 us
  local copies, waits for them, and re-layouts: 3.74 us -> 2.29 us
  other arithmetic: 1.09 us -> 0 us
    pallas_call x1, Pallas kernels: 91 us -> 87.2 us  [body(): pl.pallas_call(functools.partial(kernel, dp_ways, ctx_ways), out_shape=ja...]
    unnamed x5 -> x1, local copies, waits for them, and re-layouts: 3.59 us -> 2.29 us
where the time goes in v2:
time: 89.7 us; the launch traced here: 89.5 us
  Pallas kernels  87.2 us (97%)
  local copies, waits for them, and re-layouts  2.29 us (3%)
    pallas_call x1, Pallas kernels, body(): pl.pallas_call(functools.partial(kernel, dp_ways, ctx_ways), out_shape=ja...  87.2 us
    unnamed x1, local copies, waits for them, and re-layouts  2.29 us

profile of v2, /device:TPU:1, one launch (start us, length us, event | category | flops | bytes accessed | tf_op | source)
XLA Modules:
  0.0 89.5 jit_solution(17886746198748568626)
XLA Ops:
  0.0 87.2 %shard_map.82 = bf16[128,4096]{1,0:T(8,128)(2,1)} custom-call(s32[1,4]{1,0:T(1,128)} %doc_ref.1, s32[1,8]{1,0:T(1,128)} %slot_ref.1, bf16[512,512]{1,0:T(8,128)(2,1)} %wk_hbm.1, bf16[512,512]{1,0:T(8,128)(2,1)} %wv_hbm.1, bf16[128,4096]{1,0:T(8,128)(2,1)} %bitcast.6, f32[1,4096]{1,0:T(1,128)} %bitcast.9, bf16[128,4096]{1,0:T(8,128)(2,1)} %bitcast.7, ...), custom_call_target="tpu_custom_call" | custom-call | tf_op jit(solution)/shard_map/pallas_call | solution.py:431
  87.2 2.3 %copy.10 = bf16[1,128,4096]{2,1,0:T(8,128)(2,1)} copy(bf16[1,128,4096]{2,1,0:T(8,128)(2,1)} %bitcast.5) | data formatting | bytes 2097152

commit v3 on v2

--- a/solution.py
+++ b/solution.py
@@ -187,12 +187,23 @@
                 else:
                     arrive(h, p, other, inside)
 
-    def wave(w):
-        if w + 1 < KV_HEADS:
-            start_own(w + 1)
-        for h in range(KV_HEADS):
-            if 1 <= w - h + 1 <= line:
-                relay(h, w - h + 1)
+    steps = [
+        (h, w - h + 1)
+        for w in range(KV_HEADS + line - 1)
+        for h in range(KV_HEADS)
+        if 1 <= w - h + 1 <= line
+    ]
+
+    def relays(count):
+        for _ in range(min(count, len(steps))):
+            h, k = steps.pop(0)
+            if k == 1 and h + 1 < KV_HEADS:
+                start_own(h + 1)
+            relay(h, k)
+
+    def relays_through(h):
+        if (h, line) in steps:
+            relays(steps.index((h, line)) + 1)
 
     start_own(0)
     loads[0].wait()
@@ -204,7 +215,7 @@
         e = emb_ref[:, k * step_cols : (k + 1) * step_cols].astype(F32)
         total += jnp.sum(e * e, axis=1, keepdims=True)
     inv_rms = lax.rsqrt(total * (1.0 / dim) + 1e-05)
-    wave(0)
+    relays(1)
     for k in range(col_steps):
         cols = slice(k * step_cols, (k + 1) * step_cols)
         e = emb_ref[:, cols].astype(F32)
@@ -321,11 +332,12 @@
             dv_acc[...] += jnp.dot(half, do, preferred_element_type=F32)
             return carry
 
-        cut = GROUP // wide // 2
-        lax.fori_loop(0, cut, chunk, 0)
-        if between is not None:
-            between()
-        lax.fori_loop(cut, GROUP // wide, chunk, 0)
+        count = GROUP // wide
+        cuts = (0, count // 4, count // 2, count)
+        for first, last in zip(cuts, cuts[1:]):
+            lax.fori_loop(first, last, chunk, 0, unroll=wide > 1)
+            if between is not None and last < count:
+                between()
         gs[h, :, 0] = dk_acc[...].astype(BF16).reshape(ctx_ways, toks, HEAD)
         gs[h, :, 1] = dv_acc[...].astype(BF16).reshape(ctx_ways, toks, HEAD)
         for step in range(1, ctx_ways):
@@ -341,7 +353,7 @@
                 )
             )
 
-    def backward(h):
+    def grads(h):
         for step in range(1, ctx_ways):
             src = lax.rem(ctx + step, ctx_ways)
             pltpu.make_async_remote_copy(
@@ -366,18 +378,26 @@
             src = lax.rem(ctx + step, ctx_ways)
             own += rs[h, src, core].astype(F32)
             cross += rs[h, src, 1 - core].astype(F32)
-        own, cross = own.astype(BF16), cross.astype(BF16)
+        return [own.astype(BF16), cross.astype(BF16)]
+
+    def backward(heads):
+        left = jnp.concatenate([g for h in heads for g in grads(h)], axis=1)
+        row_total = jnp.zeros((toks, 1), F32)
         for p in range(dp_ways):
             cols = slice(p * rows, (p + 1) * rows)
-            term = lax.dot_general(own, wg[h, p], NT, preferred_element_type=F32)
-            term += lax.dot_general(cross, wo[h, p], NT, preferred_element_type=F32)
-            if h == 0:
-                gn[:, cols] = term
-            else:
-                gn[:, cols] += term
-
-    for w in range(1, line + 1):
-        wave(w)
+            right = jnp.concatenate([w[h, p] for h in heads for w in (wg, wo)], axis=1)
+            term = lax.dot_general(left, right, NT, preferred_element_type=F32)
+            if heads[0] > 0:
+                term += gn[:, cols]
+            gn[:, cols] = term
+            if heads[-1] == KV_HEADS - 1:
+                row_total += jnp.sum(
+                    emb_ref[:, cols].astype(F32) * gain_ref[:, cols] * term, axis=1, keepdims=True
+                )
+        return row_total
+
+    relays_through(0)
+    relays(2)
     complete(0)
     pltpu.make_async_remote_copy(
         src_ref=n2.at[1 - core],
@@ -389,20 +409,14 @@
     ).wait_recv()
     for h in range(KV_HEADS):
         if h > 0:
+            relays_through(h)
             complete(h)
         project(h)
-        if h >= 2:
-            backward(h - 2)
-        attend(h, functools.partial(wave, line + 1 + h))
-    backward(KV_HEADS - 2)
-    backward(KV_HEADS - 1)
-
-    total = jnp.zeros((toks, 1), F32)
-    for k in range(col_steps):
-        cols = slice(k * step_cols, (k + 1) * step_cols)
-        total += jnp.sum(
-            emb_ref[:, cols].astype(F32) * gain_ref[:, cols] * gn[:, cols], axis=1, keepdims=True
-        )
+        relays(2 if h == 0 else 1)
+        if h == KV_HEADS - 1:
+            backward(range(KV_HEADS // 2))
+        attend(h, functools.partial(relays, 1))
+    total = backward(range(KV_HEADS // 2, KV_HEADS))
     shift = inv_rms * inv_rms * inv_rms * (total * (1.0 / dim))
     for k in range(col_steps):
         cols = slice(k * step_cols, (k + 1) * step_cols)

time: 89.7 us -> 86.5 us (0.964)
  Pallas kernels: 87.2 us -> 84 us
    pallas_call x1, Pallas kernels: 87.2 us -> 84 us  [body(): pl.pallas_call(functools.partial(kernel, dp_ways, ctx_ways), out_shape=ja...]
where the time goes in v3:
time: 86.5 us; the launch traced here: 86.3 us
  Pallas kernels  84 us (97%)
  local copies, waits for them, and re-layouts  2.29 us (3%)
    pallas_call x1, Pallas kernels, body(): pl.pallas_call(functools.partial(kernel, dp_ways, ctx_ways), out_shape=ja...  84 us
    unnamed x1, local copies, waits for them, and re-layouts  2.29 us

profile of v3, /device:TPU:1, one launch (start us, length us, event | category | flops | bytes accessed | tf_op | source)
XLA Modules:
  0.0 86.3 jit_solution(4915377888250447025)
XLA Ops:
  0.0 84.0 %shard_map.82 = bf16[128,4096]{1,0:T(8,128)(2,1)} custom-call(s32[1,4]{1,0:T(1,128)} %doc_ref.1, s32[1,8]{1,0:T(1,128)} %slot_ref.1, bf16[512,512]{1,0:T(8,128)(2,1)} %wk_hbm.1, bf16[512,512]{1,0:T(8,128)(2,1)} %wv_hbm.1, bf16[128,4096]{1,0:T(8,128)(2,1)} %bitcast.6, f32[1,4096]{1,0:T(1,128)} %bitcast.9, bf16[128,4096]{1,0:T(8,128)(2,1)} %bitcast.7, ...), custom_call_target="tpu_custom_call" | custom-call | tf_op jit(solution)/shard_map/pallas_call | solution.py:445
  84.0 2.3 %copy.10 = bf16[1,128,4096]{2,1,0:T(8,128)(2,1)} copy(bf16[1,128,4096]{2,1,0:T(8,128)(2,1)} %bitcast.5) | data formatting | bytes 2097152

commit v4 on v3

--- a/solution.py
+++ b/solution.py
@@ -421,7 +421,7 @@
     for k in range(col_steps):
         cols = slice(k * step_cols, (k + 1) * step_cols)
         e = emb_ref[:, cols].astype(F32)
-        out_ref[:, cols] = (inv_rms * gain_ref[:, cols] * gn[:, cols] - e * shift).astype(BF16)
+        out_ref[:, cols] = inv_rms * gain_ref[:, cols] * gn[:, cols] - e * shift
 
     for copy, cond in sends:
         if cond is None:
@@ -444,7 +444,7 @@
     splits = 2
     out = pl.pallas_call(
         functools.partial(kernel, dp_ways, ctx_ways),
-        out_shape=jax.ShapeDtypeStruct((toks, dim), BF16),
+        out_shape=jax.ShapeDtypeStruct((toks, dim), F32),
         in_specs=[smem, smem, hbm, hbm, hbm, vmem, hbm, hbm],
         out_specs=vmem,
         scratch_shapes=[
@@ -480,7 +480,7 @@
     )(
         block_doc, slot_order, w_key, w_value, embed_rows, norm_gain[None], queries[0], d_out[0]
     )
-    return out[None]
+    return out.astype(BF16)[None]
 
 
 def solution(mesh):

time: 86.5 us -> 87.3 us (level)
  other arithmetic: 0 us -> 2.69 us
  local copies, waits for them, and re-layouts: 2.29 us -> 0 us
    broadcast_in_dim x0 -> x1, other arithmetic: none -> 2.69 us  [body(): return out.astype(BF16)[None]]
    unnamed x1 -> x0, local copies, waits for them, and re-layouts: 2.29 us -> none
where the time goes in v4:
time: 87.3 us; the launch traced here: 87.1 us
  Pallas kernels  84.4 us (97%)
  other arithmetic  2.69 us (3%)
    pallas_call x1, Pallas kernels, body(): pl.pallas_call(functools.partial(kernel, dp_ways, ctx_ways), out_shape=ja...  84.4 us
    broadcast_in_dim x1, other arithmetic, body(): return out.astype(BF16)[None]  2.69 us

profile of v4, /device:TPU:1, one launch (start us, length us, event | category | flops | bytes accessed | tf_op | source)
XLA Modules:
  0.0 87.1 jit_solution(12029869163083640946)
XLA Ops:
  0.0 84.4 %shard_map.82 = f32[128,4096]{1,0:T(8,128)} custom-call(s32[1,4]{1,0:T(1,128)} %doc_ref.1, s32[1,8]{1,0:T(1,128)} %slot_ref.1, bf16[512,512]{1,0:T(8,128)(2,1)} %wk_hbm.1, bf16[512,512]{1,0:T(8,128)(2,1)} %wv_hbm.1, bf16[128,4096]{1,0:T(8,128)(2,1)} %bitcast.6, f32[1,4096]{1,0:T(1,128)} %bitcast.9, bf16[128,4096]{1,0:T(8,128)(2,1)} %bitcast.7, ...), custom_call_target="tpu_custom_call" | custom-call | tf_op jit(solution)/shard_map/pallas_call | solution.py:445
  84.4 2.7 %convert_bitcast_fusion = bf16[1,128,4096]{2,1,0:T(8,128)(2,1)} fusion(f32[128,4096]{1,0:T(8,128)} %shard_map.82), kind=kLoop, calls=%fused_computation | loop fusion | flops 524288 | bytes 3145728 | tf_op jit(solution)/shard_map/broadcast_in_dim | solution.py:483
